TPU v7x, 32 devices: a whole 2x2x4 slice. The times are simulated.
32 devices in a mesh: groups: 2 (over y), tile: 4 (over z), segment: 2 (over core), mp: 2 (over x).
Axes of the slice: x: 2, y: 2, z: 4, core: 2. Of those that a mesh axis runs over, the one named last changes fastest.
Arguments:
- spectra: bfloat16 [2, 64, 48, 224], P(None, ('groups', 'tile')), parts along dimension 1, may hold values from -6 to 6
- valid: int32 [2, 64], P(None, 'groups'), parts along dimension 1, may hold values from 1 to 48, as said below
- project: bfloat16 [224, 16], replicated, may hold values from -0.375 to 0.375
- enc_in: bfloat16 [768, 3072], P(None, 'mp'), may hold values from -0.21875 to 0.21875
- enc_out: bfloat16 [3072, 768], P('mp'), may hold values from -0.109375 to 0.109375
- tok_embed: bfloat16 [48, 2048], replicated, may hold values from -0.875 to 0.875
- band_embed: bfloat16 [16, 2048], P('tile'), may hold values from -3 to 3
- dec_in: bfloat16 [2048, 8192], P('tile', 'mp'), may hold values from -0.125 to 0.125
- dec_out: bfloat16 [8192, 2048], P('mp', 'tile'), may hold values from -0.0625 to 0.0625
- head: bfloat16 [2048, 672], P('tile', 'mp'), may hold values from -0.125 to 0.125
Outputs:
- grad_project: float32 [448, 16], P(('groups', 'tile', 'segment')), parts along dimension 0
- grad_enc_in: float32 [1536, 3072], P(('groups', 'tile', 'segment'), 'mp'), parts along dimension 0
- grad_enc_out: float32 [6144, 768], P(('groups', 'mp'), ('tile', 'segment')), parts along dimension 0
There are 2 independent parts, one for each index of `groups`. A program takes and returns all parts, laid end to end along the dimension named above; an argument that names none is the same for every part. Nothing has to cross between parts.
Inputs may be any that keep to these rules, and one draw needn't show every extreme that they name: Pixels of patch n in micro-batch m with index below valid[m, n] count in the loss.
All inputs are finite; a program needn't handle non-finite values.
Results may differ from a plain program's by a relative error of at most 0.018.
Values may be sent and summed in bfloat16 or wider, within the bound.
A program may use at most 128 MiB of HBM per device.

v0:
```python
import jax
import jax.numpy as jnp
from jax import lax
from jax.sharding import PartitionSpec as P

BF = jnp.bfloat16
F32 = jnp.float32


def inv_rms(values):
    return lax.rsqrt(jnp.mean(values * values, axis=-1, keepdims=True) + 1e-05)


def rms_back(values, gradient):
    scaling = inv_rms(values)
    normed = values * scaling
    return scaling * (gradient - normed * jnp.mean(gradient * normed, axis=-1, keepdims=True))


def gelu(v):
    return 0.5 * v * (1 + jnp.tanh(0.7978845608028654 * (v + 0.044715 * v * v * v)))


def gelu_and_slope(v):
    square = v * v
    t = jnp.tanh(0.7978845608028654 * v * (1 + 0.044715 * square))
    half = 0.5 * (1 + t)
    slope = half + 0.5 * v * (1 - t * t) * 0.7978845608028654 * (1 + 3 * 0.044715 * square)
    return (v * half, slope)


def dot(a, b):
    return jnp.dot(a, b, preferred_element_type=F32)


def dot_t(a, b):
    return lax.dot_general(a, b, (((1,), (1,)), ((), ())), preferred_element_type=F32)


def t_dot(a, b):
    return lax.dot_general(a, b, (((0,), (0,)), ((), ())), preferred_element_type=F32)


def body(spectra, valid, project, enc_in, enc_out, tok_embed, band_embed, dec_in, dec_out, head):
    tile, seg, mp = (lax.axis_index(a) for a in ("tile", "segment", "mp"))
    T, S, M = (lax.axis_size(a) for a in ("tile", "segment", "mp"))
    batches, per_tile, pixels, bands = spectra.shape
    codes = project.shape[1]
    width = bands // codes
    local = batches * per_tile
    share = local // (S * M)
    rows = T * local
    student = codes * pixels
    dim = tok_embed.shape[1]
    dt = dec_in.shape[0]
    hid = dec_in.shape[1] // S
    once = jnp.logical_and(seg == 0, mp == 0).astype(F32)
    patches = spectra.reshape(local, pixels, bands)
    flat = patches.reshape(local * pixels, bands)
    feat_local = (
        dot(flat, project)
        .astype(BF)
        .reshape(local, pixels, codes)
        .transpose(0, 2, 1)
        .reshape(local, student)
    )
    feats = lax.all_gather(feat_local, "tile")
    feats = feats.reshape(T, S, M, share, student).transpose(1, 2, 0, 3, 4).reshape(rows, student)
    band_all = lax.all_gather(band_embed, "tile", tiled=True)
    head_full = lax.all_gather(head, "mp", axis=1, tiled=True)
    embed = jnp.concatenate([tok_embed, band_all], axis=0)
    embed_z = lax.dynamic_slice_in_dim(embed, tile * dt, dt, 1)
    d_in = lax.dynamic_slice_in_dim(dec_in, seg * hid, hid, 1)
    d_out = lax.dynamic_slice_in_dim(dec_out, seg * hid, hid, 0)
    folded = lax.psum(dot(embed_z, d_in).astype(BF), "tile")
    fold_tok, fold_band = (folded[:pixels], folded[pixels:])
    feats32 = feats.astype(F32)
    normed = (feats32 * inv_rms(feats32)).astype(BF)
    pre_act, pre_slope = gelu_and_slope(dot(normed, enc_in))
    act_out = pre_act.astype(BF)
    summed = lax.psum(dot(act_out, enc_out).astype(BF), "mp").astype(F32)
    encoded = (feats32 + summed).astype(BF)
    tokens = rows * codes
    tok = encoded.reshape(tokens, pixels)
    embedded = (
        (dot(tok, tok_embed).reshape(rows, codes, dim) + band_all.astype(F32))
        .reshape(tokens, dim)
        .astype(BF)
    )
    scaling = inv_rms(embedded.astype(F32))
    hid_pre = scaling * (
        dot(tok, fold_tok).reshape(rows, codes, hid) + fold_band.astype(F32)
    ).reshape(tokens, hid)
    hid_act, hid_slope = gelu_and_slope(hid_pre)
    embedded_z = lax.dynamic_slice_in_dim(embedded, tile * dt, dt, 1)
    decoded = (once * embedded_z.astype(F32) + dot(hid_act.astype(BF), d_out)).astype(BF)
    partial = dot(decoded, head_full).astype(BF)
    own = lax.psum_scatter(
        partial.reshape(S * M, T, share * codes, -1), ("segment", "mp"), scatter_dimension=0
    )
    own = lax.psum_scatter(own, "tile", scatter_dimension=0).astype(F32)
    quarter = (seg * M + mp) * share
    own_patches = lax.dynamic_slice_in_dim(patches, quarter, share, 0)
    target = (
        own_patches.reshape(share, pixels, codes, width)
        .transpose(0, 2, 1, 3)
        .reshape(share * codes, -1)
    )
    total_valid = jnp.sum(valid.astype(F32))
    loss_scale = 2.0 * batches * valid.shape[1] / total_valid
    own_valid = lax.dynamic_slice_in_dim(valid, tile * per_tile, per_tile, 1).reshape(local)
    own_valid = lax.dynamic_slice_in_dim(own_valid, quarter, share, 0)
    column = jnp.arange(pixels * width, dtype=jnp.int32) // width
    mask = (column[None, :] < jnp.repeat(own_valid, codes)[:, None]).astype(F32)
    grad_own = (loss_scale * mask * (own - target.astype(F32))).astype(BF)
    grad_rebuilt = lax.all_gather(lax.all_gather(grad_own, "tile"), ("segment", "mp")).reshape(
        tokens, -1
    )
    grad_decoded = dot_t(grad_rebuilt, head_full).astype(BF)
    grad_hid = hid_slope * dot_t(grad_decoded, d_out)
    tok_z = lax.dynamic_slice_in_dim(tok_embed, tile * dt, dt, 1)
    unit_tok = dot_t((embedded.astype(F32) * scaling).astype(BF), tok_embed)
    along = jnp.sum(grad_hid * hid_pre, axis=1, keepdims=True) / dim
    grad_tok = scaling * (dot_t(grad_hid.astype(BF), fold_tok) - unit_tok * along)
    grad_tok = grad_tok + once * dot_t(grad_decoded, tok_z)
    grad_encoded = lax.psum(grad_tok.reshape(rows, student).astype(BF), ("tile", "segment", "mp"))
    grad_act = (pre_slope * dot_t(grad_encoded, enc_out)).astype(BF)
    columns = student // (T * S)
    start = (tile * S + seg) * columns
    grad_out = t_dot(act_out, lax.dynamic_slice_in_dim(grad_encoded, start, columns, 1))
    grad_in = t_dot(lax.dynamic_slice_in_dim(normed, start, columns, 1), grad_act)
    grad_normed = lax.psum(dot_t(grad_act, enc_in).astype(BF), "mp").astype(F32)
    own_rows = lambda a: lax.dynamic_slice_in_dim(
        a.reshape(S * M, T, share, student), tile, 1, 1
    ).reshape(local, student)
    grad_feat = (
        own_rows(grad_encoded).astype(F32) + rms_back(feat_local.astype(F32), own_rows(grad_normed))
    ).astype(BF)
    grad_codes = grad_feat.reshape(local, codes, pixels).transpose(0, 2, 1).reshape(-1, codes)
    grad_proj = jnp.sum(lax.all_gather(t_dot(flat, grad_codes), "tile"), axis=0)
    proj_rows = bands // (T * S)
    grad_proj = lax.dynamic_slice_in_dim(grad_proj, (tile * S + seg) * proj_rows, proj_rows, 0)
    return (grad_proj, grad_in, grad_out)


def solution(mesh):
    placed = (
        P(None, ("groups", "tile"), None, None),
        P(None, "groups"),
        P(),
        P(None, "mp"),
        P("mp", None),
        P(),
        P("tile", None),
        P("tile", "mp"),
        P("mp", "tile"),
        P("tile", "mp"),
    )
    return jax.shard_map(
        body,
        mesh=mesh,
        in_specs=placed,
        out_specs=(
            P(("groups", "tile", "segment"), None),
            P(("groups", "tile", "segment"), "mp"),
            P(("groups", "mp"), ("tile", "segment")),
        ),
        check_vma=False,
    )
```

profile of v0, /device:TPU:0, one launch (start us, length us, event | category | flops | bytes accessed | tf_op | source)
XLA Modules:
  0.0 350.5 jit_solution(10092934858017082224)
XLA Ops:
  9.6 15.0 %all_gather.25 = bf16[4,16,768]{2,1,0:T(8,128)(2,1)S(1)} all-gather(bf16[1,16,768]{2,1,0:T(8,128)(2,1)S(1)} %all_gather_reshape.3), channel_id=1, replica_groups=mesh['groups'=2,'tile'=4,'segment'=2,'mp'=2] {'tile'}, dimensions={0}, use_global_device_ids=true | all-gather | bytes 122880 | tf_op jit(solution)/shard_map/all_gather | solution.py:67
  25.2 2.2 fusion.50
  29.5 13.3 %all-gather.2 = bf16[4,4,2048]{2,1,0:T(4,128)(2,1)S(1)} all-gather(bf16[1,4,2048]{2,1,0:T(4,128)(2,1)S(1)} %bitcast.88), channel_id=1, replica_groups=mesh['groups'=2,'tile'=4,'segment'=2,'mp'=2] {'tile'}, dimensions={0}, use_global_device_ids=true | all-gather | bytes 81920 | tf_op jit(solution)/shard_map/all_gather | solution.py:69
  42.8 2.8 convolution_convert_fusion
  46.4 8.4 %all_gather.27 = bf16[512,672]{0,1:T(8,128)(2,1)S(1)} all-gather(bf16[512,336]{0,1:T(8,128)(2,1)} %param.19), channel_id=1, replica_groups=mesh['groups'=2,'tile'=4,'segment'=2,'mp'=2] {'mp'}, dimensions={1}, use_global_device_ids=true | all-gather | bytes 1032192 | tf_op jit(solution)/shard_map/all_gather | solution.py:70
  56.1 4.2 %multiply_reduce_fusion.1 = (f32[64,16]{1,0:T(8,128)S(1)}, bf16[64,16,2048]{2,1,0:T(8,128)(2,1)}) fusion(f32[16,2048]{1,0:T(8,128)} %convert_element_type.165, bf16[64,16,48]{2,1,0:T(8,128)(2,1)S(1)} %dot_general.61, bf16[48,2048]{1,0:T(8,128)(2,1)} %param.15), kind=kOutput, calls=%fused_computation.7 | convolution fusion | flops 211811328 | bytes 4624384 | tf_op jit(solution)/shard_map/dot_general | solution.py:33
  60.4 29.6 %all-reduce.7.cloned.1.call-done = bf16[64,2048]{1,0:T(8,128)(2,1)} async-done(((bf16[64,2048]{1,0:T(8,128)(2,1)}), bf16[64,2048]{1,0:T(8,128)(2,1)}) %all-reduce.7.cloned.1.call-update) | async-done | bytes 262160 | tf_op jit(solution)/shard_map/psum | solution.py:75
  90.8 2.2 convolution_add_fusion
  93.0 5.3 %multiply_convert_fusion.1 = bf16[1024,2048]{1,0:T(8,128)(2,1)} fusion(f32[64,16,2048]{2,1,0:T(8,128)S(1)} %convolution_add_fusion, f32[1024]{0:T(1024)S(1)} %rsqrt.37), kind=kLoop, calls=%fused_computation.3 | loop fusion | flops 20971520 | bytes 12587008 | tf_op jit(solution)/shard_map/convert_element_type | solution.py:96
  98.3 7.2 %convolution_convert_fusion.1 = bf16[1024,672]{0,1:T(8,128)(2,1)} fusion(bf16[512,672]{0,1:T(8,128)(2,1)S(1)} %all_gather.27, bf16[1024,2048]{1,0:T(8,128)(2,1)} %multiply_convert_fusion.1, bf16[4096,512]{1,0:T(8,128)(2,1)} %param.18, s32[]{:T(128)S(6)} %select_n.37, bf16[1024,2048]{1,0:T(8,128)(2,1)} %bitcast.90, s32[]{:T(128)S(6)} %select_n.36, ...), kind=kOutput, calls=%fused_computation.22 | convolution fusion | flops 2854912000 | bytes 9404428 | tf_op jit(solution)/shard_map/dot_general | solution.py:33
  105.5 2.6 copy.40
  108.2 28.0 %reduce-scatter.3.cloned.1.call-done = bf16[1,4,64,672]{3,2,1,0:T(8,128)(2,1)} async-done(((bf16[4,4,64,672]{3,2,1,0:T(8,128)(2,1)}), bf16[1,4,64,672]{3,2,1,0:T(8,128)(2,1)}) %reduce-scatter.3.cloned.1.call-update) | async-done | bytes 344080 | tf_op jit(solution)/shard_map/reduce_scatter | solution.py:98
  138.7 1.9 reshape.268
  142.0 17.0 %reduce-scatter.5.cloned.1.call-done = bf16[1,64,672]{2,1,0:T(8,128)(2,1)} async-done(((bf16[4,64,672]{2,1,0:T(8,128)(2,1)}), bf16[1,64,672]{2,1,0:T(8,128)(2,1)}) %reduce-scatter.5.cloned.1.call-update) | async-done | bytes 86032 | tf_op jit(solution)/shard_map/reduce_scatter | solution.py:101
  160.0 15.8 %all_gather.28 = bf16[4,64,672]{2,1,0:T(8,128)(2,1)} all-gather(bf16[1,64,672]{2,1,0:T(8,128)(2,1)S(1)} %multiply_convert_fusion.6), channel_id=1, replica_groups=mesh['groups'=2,'tile'=4,'segment'=2,'mp'=2] {'tile'}, dimensions={0}, use_global_device_ids=true | all-gather | bytes 430080 | tf_op jit(solution)/shard_map/all_gather | solution.py:116
  176.2 17.2 %all-gather.6.cloned.1.call-done = bf16[16,64,672]{2,1,0:T(8,128)(2,1)} async-done(((bf16[4,64,672]{2,1,0:T(8,128)(2,1)}), bf16[16,64,672]{2,1,0:T(8,128)(2,1)}) %all-gather.6.cloned.1.call-update) | async-done | bytes 1376272 | tf_op jit(solution)/shard_map/all_gather | solution.py:116
  193.4 2.7 convolution_convert_fusion.2
  196.3 9.2 %multiply_reduce_fusion = (f32[1024]{0:T(1024)S(1)}, bf16[1024,2048]{1,0:T(8,128)(2,1)S(1)}) fusion(f32[64,16,2048]{2,1,0:T(8,128)} %copy-done.1, f32[1024]{0:T(1024)S(1)} %rsqrt.37, bf16[1024,512]{1,0:T(8,128)(2,1)S(1)} %convolution_convert_fusion.2, bf16[4096,512]{1,0:T(8,128)(2,1)S(1)} %copy-done.12, s32[]{:T(128)S(6)} %select_n.37), kind=kOutput, calls=%fused_computation.1 | convolution fusion | flops 2191522816 | bytes 15736836 | tf_op jit(solution)/shard_map/dot_general | solution.py:37
  207.5 2.0 fusion.21
  212.7 86.1 %all-reduce.9.cloned.1.call-done = bf16[64,768]{1,0:T(8,128)(2,1)} async-done(((bf16[64,768]{1,0:T(8,128)(2,1)}), bf16[64,768]{1,0:T(8,128)(2,1)}) %all-reduce.9.cloned.1.call-update) | async-done | bytes 98320 | tf_op jit(solution)/shard_map/psum | solution.py:126
  300.5 3.1 convolution_convert_fusion.3
  307.2 1.9 fusion.34
  310.2 17.2 %all-reduce.11.cloned.1.call-done = bf16[4,4,4,768]{3,2,0,1:T(4,128)(2,1)} async-done(((bf16[4,4,4,768]{3,2,0,1:T(4,128)(2,1)}), bf16[4,4,4,768]{3,2,0,1:T(4,128)(2,1)}) %all-reduce.11.cloned.1.call-update) | async-done | bytes 98320 | tf_op jit(solution)/shard_map/psum | solution.py:132
  329.7 13.3 %all-gather.3 = f32[4,224,16]{1,2,0:T(8,128)S(1)} all-gather(f32[1,224,16]{1,2,0:T(8,128)S(1)} %convolution_bitcast_fusion), channel_id=3, replica_groups=mesh['groups'=2,'tile'=4,'segment'=2,'mp'=2] {'tile'}, dimensions={0}, use_global_device_ids=true | all-gather | bytes 71680 | tf_op jit(solution)/shard_map/all_gather | solution.py:140
  (102 shorter events, 26.9 us)
Async XLA Ops:
  7.2 21.0 %copy-start = (bf16[1536,768]{1,0:T(8,128)(2,1)S(1)}, bf16[1536,768]{1,0:T(8,128)(2,1)}, u32[]{:S(2)}) copy-start(bf16[1536,768]{1,0:T(8,128)(2,1)} %param.14) | copy-start | bytes 7077892
  7.2 22.3 %copy-start.10 = (bf16[4,2048]{1,0:T(4,128)(2,1)S(1)}, bf16[4,2048]{1,0:T(4,128)(2,1)}, u32[]{:S(2)}) copy-start(bf16[4,2048]{1,0:T(4,128)(2,1)} %param.16) | copy-start | bytes 49156
  7.2 47.6 %all-reduce.5.cloned.1.call-start = ((), (), s32[]{:S(2)}) async-start(), calls=%async_computation.2 | async-start | bytes 196608 | tf_op jit(solution)/shard_map/psum | solution.py:81
  7.2 35.6 %copy-start.8 = (bf16[48,2048]{1,0:T(8,128)(2,1)S(1)}, bf16[48,2048]{1,0:T(8,128)(2,1)}, u32[]{:S(2)}) copy-start(bf16[48,2048]{1,0:T(8,128)(2,1)} %param.15) | copy-start | bytes 589828
  25.2 4.3 %copy-start.7 = (bf16[64,768]{1,0:T(8,128)(2,1)}, bf16[64,768]{1,0:T(8,128)(2,1)S(1)}, u32[]{:S(2)}) copy-start(bf16[64,768]{1,0:T(8,128)(2,1)S(1)} %multiply_convert_fusion.7) | copy-start | bytes 294916
  27.4 0.8 copy-start.3
  29.4 60.6 %all-reduce.7.cloned.1.call-start = ((), (), s32[]{:S(2)}) async-start(), calls=%async_computation.3 | async-start | bytes 524288 | tf_op jit(solution)/shard_map/psum | solution.py:75
  45.6 90.6 %reduce-scatter.3.cloned.1.call-start = ((), (), s32[]{:S(2)}) async-start(), calls=%async_computation.4 | async-start | bytes 1966080 | tf_op jit(solution)/shard_map/reduce_scatter | solution.py:98
  54.7 43.5 %copy-start.6 = (bf16[512,672]{0,1:T(8,128)(2,1)}, bf16[512,672]{0,1:T(8,128)(2,1)S(1)}, u32[]{:S(2)}) copy-start(bf16[512,672]{0,1:T(8,128)(2,1)S(1)} %all_gather.27) | copy-start | bytes 2064388
  93.0 5.3 %copy-start.1 = (f32[64,16,2048]{2,1,0:T(8,128)}, f32[64,16,2048]{2,1,0:T(8,128)S(1)}, u32[]{:S(2)}) copy-start(f32[64,16,2048]{2,1,0:T(8,128)S(1)} %convolution_add_fusion) | copy-start | bytes 25165828
  105.5 30.8 %copy-start.11 = (s32[2,32]{1,0:T(2,128)S(1)}, s32[2,32]{1,0:T(2,128)}, u32[]{:S(2)}) copy-start(s32[2,32]{1,0:T(2,128)} %param.11) | copy-start | bytes 772
  105.5 31.2 %copy-start.2 = (bf16[2,8,48,224]{3,2,1,0:T(8,128)(2,1)S(1)}, bf16[2,8,48,224]{3,2,1,0:T(8,128)(2,1)}, u32[]{:S(2)}) copy-start(bf16[2,8,48,224]{3,2,1,0:T(8,128)(2,1)} %param.10) | copy-start | bytes 1032196
  108.1 50.8 %reduce-scatter.5.cloned.1.call-start = ((), (), s32[]{:S(2)}) async-start(), calls=%async_computation.5 | async-start | bytes 491520 | tf_op jit(solution)/shard_map/reduce_scatter | solution.py:101
  136.2 57.2 %all-gather.6.cloned.1.call-start = ((), (), s32[]{:S(2)}) async-start(), calls=%async_computation.8 | async-start | bytes 1966080 | tf_op jit(solution)/shard_map/all_gather | solution.py:116
  175.8 123.0 %all-reduce.9.cloned.1.call-start = ((), (), s32[]{:S(2)}) async-start(), calls=%async_computation.6 | async-start | bytes 196608 | tf_op jit(solution)/shard_map/psum | solution.py:126
  193.4 2.9 copy-start.12
  196.3 9.2 %copy-start.9 = (bf16[48,2048]{1,0:T(8,128)(2,1)S(1)}, bf16[48,2048]{1,0:T(8,128)(2,1)}, u32[]{:S(2)}) copy-start(bf16[48,2048]{1,0:T(8,128)(2,1)} %param.15) | copy-start | bytes 589828
  196.3 9.7 %copy-start.13 = (bf16[64,16,2048]{2,1,0:T(8,128)(2,1)S(1)}, bf16[64,16,2048]{2,1,0:T(8,128)(2,1)}, u32[]{:S(2)}) copy-start(bf16[64,16,2048]{2,1,0:T(8,128)(2,1)} %get-tuple-element.6) | copy-start | bytes 12582916
  206.0 1.5 copy-start.5
  207.5 91.4 %copy-start.4 = (f32[64,1536]{1,0:T(8,128)S(1)}, f32[64,1536]{1,0:T(8,128)}, u32[]{:S(2)}) copy-start(f32[64,1536]{1,0:T(8,128)} %copy-done.3) | copy-start | bytes 1179652
  211.5 115.9 %all-reduce.11.cloned.1.call-start = ((), (), s32[]{:S(2)}) async-start(), calls=%async_computation.7 | async-start | bytes 196608 | tf_op jit(solution)/shard_map/psum | solution.py:132
Sparse Core Ops, SparseCore 0:
  29.5 22.1 all-reduce.4
  54.6 35.3 all-reduce.6
  108.3 27.9 reduce-scatter.2
  138.3 20.5 reduce-scatter.4
  175.9 17.4 all-gather.5
  211.6 87.1 all-reduce.8
  307.3 20.0 all-reduce.10
where the time goes:
time: 351 us; the launch traced here: 350 us
  waiting for transfers between devices  195 us (56%)
  blocking collectives  65.8 us (19%)
  matrix products  45.8 us (13%)
  local copies, waits for them, and re-layouts  15.7 us (4%)
  between operations  15.2 us (4%)
  other arithmetic  12.3 us (4%)
    psum x1, waiting for transfers between devices, body(): lax.psum(grad_tok.reshape(rows, student).astype(BF), ('tile', 'segment',...  86.1 us
    psum x1, waiting for transfers between devices, body(): folded = lax.psum(dot(embed_z, d_in).astype(BF), 'tile')  29.6 us
    reduce_scatter x1, waiting for transfers between devices, body(): lax.psum_scatter(partial.reshape(S * M, T, share * codes, -1), ('segment'...  28 us
    dot_general x7, matrix products, dot(): return jnp.dot(a, b, preferred_element_type=F32)  21.1 us
    dot_general x7, matrix products, dot_t(): lax.dot_general(a, b, (((1,), (1,)), ((), ())), preferred_element_type=F32)  20.7 us
    all_gather x1, waiting for transfers between devices, body(): lax.all_gather(lax.all_gather(grad_own, 'tile'), ('segment', 'mp'))  17.2 us
    psum x1, waiting for transfers between devices, body(): grad_normed = lax.psum(dot_t(grad_act, enc_in).astype(BF), 'mp').astype(F32)  17.2 us
    reduce_scatter x1, waiting for transfers between devices, body(): own = lax.psum_scatter(own, 'tile', scatter_dimension=0).astype(F32)  17 us
  transfers between devices with their start and end apart: 7, of which 6 were waited for; matrix products, arithmetic and copies ran while one was open for 5% of the time, Pallas kernels for 0%

commit v1 on v0

--- a/solution.py
+++ b/solution.py
@@ -123,7 +123,9 @@
     along = jnp.sum(grad_hid * hid_pre, axis=1, keepdims=True) / dim
     grad_tok = scaling * (dot_t(grad_hid.astype(BF), fold_tok) - unit_tok * along)
     grad_tok = grad_tok + once * dot_t(grad_decoded, tok_z)
-    grad_encoded = lax.psum(grad_tok.reshape(rows, student).astype(BF), ("tile", "segment", "mp"))
+    grad_encoded = lax.psum(
+        lax.psum(grad_tok.reshape(rows, student).astype(BF), ("segment", "mp")), "tile"
+    )
     grad_act = (pre_slope * dot_t(grad_encoded, enc_out)).astype(BF)
     columns = student // (T * S)
     start = (tile * S + seg) * columns

time: 351 us -> 333 us (0.949)
  waiting for transfers between devices: 195 us -> 177 us
    psum x1 -> x2, waiting for transfers between devices: 86.1 us -> 66.5 us  [the longest x1 35.4 us: body(): lax.psum(lax.psum(grad_tok.reshape(rows, student).astype(BF), ('segment',...]
  transfers between devices with their start and end apart: 7 -> 8, of which waited for: 6 -> 7; matrix products, arithmetic and copies ran while one was open for 5% -> 6% of each run, Pallas kernels for 0% -> 0%
where the time goes in v1:
time: 333 us; the launch traced here: 332 us
  waiting for transfers between devices  177 us (53%)
  blocking collectives  65.8 us (20%)
  matrix products  45.8 us (14%)
  local copies, waits for them, and re-layouts  15.7 us (5%)
  between operations  15.2 us (5%)
  other arithmetic  12.3 us (4%)
    psum x1, waiting for transfers between devices, body(): lax.psum(lax.psum(grad_tok.reshape(rows, student).astype(BF), ('segment',...  35.4 us
    psum x1, waiting for transfers between devices, body(): lax.psum(grad_tok.reshape(rows, student).astype(BF), ('segment', 'mp'))  31.1 us
    psum x1, waiting for transfers between devices, body(): folded = lax.psum(dot(embed_z, d_in).astype(BF), 'tile')  29.6 us
    reduce_scatter x1, waiting for transfers between devices, body(): lax.psum_scatter(partial.reshape(S * M, T, share * codes, -1), ('segment'...  28 us
    dot_general x7, matrix products, dot(): return jnp.dot(a, b, preferred_element_type=F32)  21.1 us
    dot_general x7, matrix products, dot_t(): lax.dot_general(a, b, (((1,), (1,)), ((), ())), preferred_element_type=F32)  20.7 us
    psum x1, waiting for transfers between devices, body(): grad_normed = lax.psum(dot_t(grad_act, enc_in).astype(BF), 'mp').astype(F32)  17.9 us
    all_gather x1, waiting for transfers between devices, body(): lax.all_gather(lax.all_gather(grad_own, 'tile'), ('segment', 'mp'))  17.4 us
  transfers between devices with their start and end apart: 8, of which 7 were waited for; matrix products, arithmetic and copies ran while one was open for 6% of the time, Pallas kernels for 0%

profile of v1, /device:TPU:0, one launch (start us, length us, event | category | flops | bytes accessed | tf_op | source)
XLA Modules:
  0.0 331.8 jit_solution(18238731493559589069)
XLA Ops:
  9.6 15.0 %all_gather.25 = bf16[4,16,768]{2,1,0:T(8,128)(2,1)S(1)} all-gather(bf16[1,16,768]{2,1,0:T(8,128)(2,1)S(1)} %all_gather_reshape.3), channel_id=1, replica_groups=mesh['groups'=2,'tile'=4,'segment'=2,'mp'=2] {'tile'}, dimensions={0}, use_global_device_ids=true | all-gather | bytes 122880 | tf_op jit(solution)/shard_map/all_gather | solution.py:67
  25.2 2.2 fusion.50
  29.5 13.3 %all-gather.2 = bf16[4,4,2048]{2,1,0:T(4,128)(2,1)S(1)} all-gather(bf16[1,4,2048]{2,1,0:T(4,128)(2,1)S(1)} %bitcast.88), channel_id=1, replica_groups=mesh['groups'=2,'tile'=4,'segment'=2,'mp'=2] {'tile'}, dimensions={0}, use_global_device_ids=true | all-gather | bytes 81920 | tf_op jit(solution)/shard_map/all_gather | solution.py:69
  42.8 2.8 convolution_convert_fusion
  46.4 8.4 %all_gather.27 = bf16[512,672]{0,1:T(8,128)(2,1)S(1)} all-gather(bf16[512,336]{0,1:T(8,128)(2,1)} %param.19), channel_id=1, replica_groups=mesh['groups'=2,'tile'=4,'segment'=2,'mp'=2] {'mp'}, dimensions={1}, use_global_device_ids=true | all-gather | bytes 1032192 | tf_op jit(solution)/shard_map/all_gather | solution.py:70
  56.1 4.2 %multiply_reduce_fusion.1 = (f32[64,16]{1,0:T(8,128)S(1)}, bf16[64,16,2048]{2,1,0:T(8,128)(2,1)}) fusion(f32[16,2048]{1,0:T(8,128)} %convert_element_type.165, bf16[64,16,48]{2,1,0:T(8,128)(2,1)S(1)} %dot_general.61, bf16[48,2048]{1,0:T(8,128)(2,1)} %param.15), kind=kOutput, calls=%fused_computation.7 | convolution fusion | flops 211811328 | bytes 4624384 | tf_op jit(solution)/shard_map/dot_general | solution.py:33
  60.4 29.6 %all-reduce.8.cloned.1.call-done = bf16[64,2048]{1,0:T(8,128)(2,1)} async-done(((bf16[64,2048]{1,0:T(8,128)(2,1)}), bf16[64,2048]{1,0:T(8,128)(2,1)}) %all-reduce.8.cloned.1.call-update) | async-done | bytes 262160 | tf_op jit(solution)/shard_map/psum | solution.py:75
  90.8 2.2 convolution_add_fusion
  93.0 5.3 %multiply_convert_fusion.1 = bf16[1024,2048]{1,0:T(8,128)(2,1)} fusion(f32[64,16,2048]{2,1,0:T(8,128)S(1)} %convolution_add_fusion, f32[1024]{0:T(1024)S(1)} %rsqrt.37), kind=kLoop, calls=%fused_computation.3 | loop fusion | flops 20971520 | bytes 12587008 | tf_op jit(solution)/shard_map/convert_element_type | solution.py:96
  98.3 7.2 %convolution_convert_fusion.1 = bf16[1024,672]{0,1:T(8,128)(2,1)} fusion(bf16[512,672]{0,1:T(8,128)(2,1)S(1)} %all_gather.27, bf16[1024,2048]{1,0:T(8,128)(2,1)} %multiply_convert_fusion.1, bf16[4096,512]{1,0:T(8,128)(2,1)} %param.18, s32[]{:T(128)S(6)} %select_n.37, bf16[1024,2048]{1,0:T(8,128)(2,1)} %bitcast.90, s32[]{:T(128)S(6)} %select_n.36, ...), kind=kOutput, calls=%fused_computation.22 | convolution fusion | flops 2854912000 | bytes 9404428 | tf_op jit(solution)/shard_map/dot_general | solution.py:33
  105.5 2.6 copy.40
  108.2 28.0 %reduce-scatter.3.cloned.1.call-done = bf16[1,4,64,672]{3,2,1,0:T(8,128)(2,1)} async-done(((bf16[4,4,64,672]{3,2,1,0:T(8,128)(2,1)}), bf16[1,4,64,672]{3,2,1,0:T(8,128)(2,1)}) %reduce-scatter.3.cloned.1.call-update) | async-done | bytes 344080 | tf_op jit(solution)/shard_map/reduce_scatter | solution.py:98
  138.7 1.9 reshape.268
  142.0 17.0 %reduce-scatter.5.cloned.1.call-done = bf16[1,64,672]{2,1,0:T(8,128)(2,1)} async-done(((bf16[4,64,672]{2,1,0:T(8,128)(2,1)}), bf16[1,64,672]{2,1,0:T(8,128)(2,1)}) %reduce-scatter.5.cloned.1.call-update) | async-done | bytes 86032 | tf_op jit(solution)/shard_map/reduce_scatter | solution.py:101
  160.0 15.8 %all_gather.28 = bf16[4,64,672]{2,1,0:T(8,128)(2,1)} all-gather(bf16[1,64,672]{2,1,0:T(8,128)(2,1)S(1)} %multiply_convert_fusion.6), channel_id=1, replica_groups=mesh['groups'=2,'tile'=4,'segment'=2,'mp'=2] {'tile'}, dimensions={0}, use_global_device_ids=true | all-gather | bytes 430080 | tf_op jit(solution)/shard_map/all_gather | solution.py:116
  176.0 17.4 %all-gather.6.cloned.1.call-done = bf16[16,64,672]{2,1,0:T(8,128)(2,1)} async-done(((bf16[4,64,672]{2,1,0:T(8,128)(2,1)}), bf16[16,64,672]{2,1,0:T(8,128)(2,1)}) %all-gather.6.cloned.1.call-update) | async-done | bytes 1376272 | tf_op jit(solution)/shard_map/all_gather | solution.py:116
  193.4 2.7 convolution_convert_fusion.2
  196.3 9.2 %multiply_reduce_fusion = (f32[1024]{0:T(1024)S(1)}, bf16[1024,2048]{1,0:T(8,128)(2,1)S(1)}) fusion(f32[64,16,2048]{2,1,0:T(8,128)} %copy-done.1, f32[1024]{0:T(1024)S(1)} %rsqrt.37, bf16[1024,512]{1,0:T(8,128)(2,1)S(1)} %convolution_convert_fusion.2, bf16[4096,512]{1,0:T(8,128)(2,1)S(1)} %copy-done.12, s32[]{:T(128)S(6)} %select_n.37), kind=kOutput, calls=%fused_computation.1 | convolution fusion | flops 2191522816 | bytes 15736836 | tf_op jit(solution)/shard_map/dot_general | solution.py:37
  207.5 2.0 fusion.21
  211.8 31.1 %all-reduce.10.cloned.1.call-done = bf16[64,768]{1,0:T(8,128)(2,1)} async-done(((bf16[64,768]{1,0:T(8,128)(2,1)}), bf16[64,768]{1,0:T(8,128)(2,1)}) %all-reduce.10.cloned.1.call-update) | async-done | bytes 98320 | tf_op jit(solution)/shard_map/psum | solution.py:127
  244.1 35.4 %all-reduce.12.cloned.1.call-done = bf16[64,768]{1,0:T(8,128)(2,1)} async-done(((bf16[64,768]{1,0:T(8,128)(2,1)}), bf16[64,768]{1,0:T(8,128)(2,1)}) %all-reduce.12.cloned.1.call-update) | async-done | bytes 98320 | tf_op jit(solution)/shard_map/psum | solution.py:126
  281.2 3.1 convolution_convert_fusion.3
  290.9 17.9 %all-reduce.14.cloned.1.call-done = bf16[4,4,4,768]{3,2,0,1:T(4,128)(2,1)} async-done(((bf16[4,4,4,768]{3,2,0,1:T(4,128)(2,1)}), bf16[4,4,4,768]{3,2,0,1:T(4,128)(2,1)}) %all-reduce.14.cloned.1.call-update) | async-done | bytes 98320 | tf_op jit(solution)/shard_map/psum | solution.py:134
  311.0 13.3 %all-gather.3 = f32[4,224,16]{1,2,0:T(8,128)S(1)} all-gather(f32[1,224,16]{1,2,0:T(8,128)S(1)} %convolution_bitcast_fusion), channel_id=3, replica_groups=mesh['groups'=2,'tile'=4,'segment'=2,'mp'=2] {'tile'}, dimensions={0}, use_global_device_ids=true | all-gather | bytes 71680 | tf_op jit(solution)/shard_map/all_gather | solution.py:142
  (105 shorter events, 28.9 us)
Async XLA Ops:
  7.2 21.0 %copy-start = (bf16[1536,768]{1,0:T(8,128)(2,1)S(1)}, bf16[1536,768]{1,0:T(8,128)(2,1)}, u32[]{:S(2)}) copy-start(bf16[1536,768]{1,0:T(8,128)(2,1)} %param.14) | copy-start | bytes 7077892
  7.2 22.3 %copy-start.10 = (bf16[4,2048]{1,0:T(4,128)(2,1)S(1)}, bf16[4,2048]{1,0:T(4,128)(2,1)}, u32[]{:S(2)}) copy-start(bf16[4,2048]{1,0:T(4,128)(2,1)} %param.16) | copy-start | bytes 49156
  7.2 47.6 %all-reduce.6.cloned.1.call-start = ((), (), s32[]{:S(2)}) async-start(), calls=%async_computation.2 | async-start | bytes 196608 | tf_op jit(solution)/shard_map/psum | solution.py:81
  7.2 35.6 %copy-start.8 = (bf16[48,2048]{1,0:T(8,128)(2,1)S(1)}, bf16[48,2048]{1,0:T(8,128)(2,1)}, u32[]{:S(2)}) copy-start(bf16[48,2048]{1,0:T(8,128)(2,1)} %param.15) | copy-start | bytes 589828
  25.2 4.3 %copy-start.7 = (bf16[64,768]{1,0:T(8,128)(2,1)}, bf16[64,768]{1,0:T(8,128)(2,1)S(1)}, u32[]{:S(2)}) copy-start(bf16[64,768]{1,0:T(8,128)(2,1)S(1)} %multiply_convert_fusion.7) | copy-start | bytes 294916
  27.4 0.8 copy-start.3
  29.4 60.6 %all-reduce.8.cloned.1.call-start = ((), (), s32[]{:S(2)}) async-start(), calls=%async_computation.3 | async-start | bytes 524288 | tf_op jit(solution)/shard_map/psum | solution.py:75
  45.6 90.6 %reduce-scatter.3.cloned.1.call-start = ((), (), s32[]{:S(2)}) async-start(), calls=%async_computation.4 | async-start | bytes 1966080 | tf_op jit(solution)/shard_map/reduce_scatter | solution.py:98
  54.7 43.5 %copy-start.6 = (bf16[512,672]{0,1:T(8,128)(2,1)}, bf16[512,672]{0,1:T(8,128)(2,1)S(1)}, u32[]{:S(2)}) copy-start(bf16[512,672]{0,1:T(8,128)(2,1)S(1)} %all_gather.27) | copy-start | bytes 2064388
  93.0 5.3 %copy-start.1 = (f32[64,16,2048]{2,1,0:T(8,128)}, f32[64,16,2048]{2,1,0:T(8,128)S(1)}, u32[]{:S(2)}) copy-start(f32[64,16,2048]{2,1,0:T(8,128)S(1)} %convolution_add_fusion) | copy-start | bytes 25165828
  105.5 30.8 %copy-start.11 = (s32[2,32]{1,0:T(2,128)S(1)}, s32[2,32]{1,0:T(2,128)}, u32[]{:S(2)}) copy-start(s32[2,32]{1,0:T(2,128)} %param.11) | copy-start | bytes 772
  105.5 31.2 %copy-start.2 = (bf16[2,8,48,224]{3,2,1,0:T(8,128)(2,1)S(1)}, bf16[2,8,48,224]{3,2,1,0:T(8,128)(2,1)}, u32[]{:S(2)}) copy-start(bf16[2,8,48,224]{3,2,1,0:T(8,128)(2,1)} %param.10) | copy-start | bytes 1032196
  108.1 50.8 %reduce-scatter.5.cloned.1.call-start = ((), (), s32[]{:S(2)}) async-start(), calls=%async_computation.5 | async-start | bytes 491520 | tf_op jit(solution)/shard_map/reduce_scatter | solution.py:101
  136.2 57.2 %all-gather.6.cloned.1.call-start = ((), (), s32[]{:S(2)}) async-start(), calls=%async_computation.9 | async-start | bytes 1966080 | tf_op jit(solution)/shard_map/all_gather | solution.py:116
  175.8 67.1 %all-reduce.10.cloned.1.call-start = ((), (), s32[]{:S(2)}) async-start(), calls=%async_computation.6 | async-start | bytes 196608 | tf_op jit(solution)/shard_map/psum | solution.py:127
  193.4 2.9 copy-start.12
  196.3 9.2 %copy-start.9 = (bf16[48,2048]{1,0:T(8,128)(2,1)S(1)}, bf16[48,2048]{1,0:T(8,128)(2,1)}, u32[]{:S(2)}) copy-start(bf16[48,2048]{1,0:T(8,128)(2,1)} %param.15) | copy-start | bytes 589828
  196.3 9.7 %copy-start.13 = (bf16[64,16,2048]{2,1,0:T(8,128)(2,1)S(1)}, bf16[64,16,2048]{2,1,0:T(8,128)(2,1)}, u32[]{:S(2)}) copy-start(bf16[64,16,2048]{2,1,0:T(8,128)(2,1)} %get-tuple-element.6) | copy-start | bytes 12582916
  206.0 1.5 copy-start.5
  207.5 72.1 %copy-start.4 = (f32[64,1536]{1,0:T(8,128)S(1)}, f32[64,1536]{1,0:T(8,128)}, u32[]{:S(2)}) copy-start(f32[64,1536]{1,0:T(8,128)} %copy-done.3) | copy-start | bytes 1179652
  211.5 68.0 %all-reduce.12.cloned.1.call-start = ((), (), s32[]{:S(2)}) async-start(), calls=%async_computation.7 | async-start | bytes 196608 | tf_op jit(solution)/shard_map/psum | solution.py:126
  242.9 65.8 %all-reduce.14.cloned.1.call-start = ((), (), s32[]{:S(2)}) async-start(), calls=%async_computation.8 | async-start | bytes 196608 | tf_op jit(solution)/shard_map/psum | solution.py:134
Sparse Core Ops, SparseCore 0:
  29.5 22.1 all-reduce.5
  54.6 35.3 all-reduce.7
  108.3 27.9 reduce-scatter.2
  138.3 20.5 reduce-scatter.4
  175.9 17.4 all-gather.5
  211.6 31.2 all-reduce.9
  245.2 34.2 all-reduce.11
  288.0 20.6 all-reduce.13
